TPU v7x, 256 devices: a whole 4x4x8 slice. The times are simulated.
256 devices in a mesh: wide: 64 (over y, z_hi, x), narrow: 4 (over z_lo, core).
Axes of the slice: x: 4, y: 4, z: 8 (z_hi: 4, z_lo: 2; z = z_hi * 2 + z_lo), core: 2. Of those that a mesh axis runs over, the one named last changes fastest.
Arguments:
- sources: bfloat16 [524288, 512], P(('wide', 'narrow')), may hold values from -6 to 6
- order: int32 [524288], P(('wide', 'narrow')), may hold values from 0 to 524287, as said below
- near_cols: int32 [4096, 8], P(('wide', 'narrow')), may hold values from 0 to 4095, as said below
- near_blocks: bfloat16 [4096, 8, 128, 128], P(('wide', 'narrow')), may hold values from -0.1875 to 0.1875
- in_basis: bfloat16 [524288, 256], P(('wide', 'narrow')), may hold values from -0.0625 to 0.0625
- transfer: bfloat16 [4, 64, 2, 256, 256], P(None, 'wide'), may hold values from -0.25 to 0.25
- out_basis: bfloat16 [524288, 256], P(('wide', 'narrow')), may hold values from -0.375 to 0.375
Outputs:
- potential: bfloat16 [524288, 512], P(('wide', 'narrow'))
Inputs may be any that keep to these rules, and one draw needn't show every extreme that they name: order maps each aligned run of 2048 rows onto itself, each row once. `near_cols`: each row block r lists distinct offsets from -4 to 4; the id is r plus the offset, clamped into r's cluster of 64 blocks.
All inputs are finite; a program needn't handle non-finite values.
Results may differ from a plain program's by a relative error of at most 0.014.
Values may be sent and summed in bfloat16 or wider, within the bound.
A program may use at most 128 MiB of HBM per device.

v0:
```python
import jax
import jax.numpy as jnp
from jax import lax
from jax.sharding import PartitionSpec as P

LEVELS = 4
REACH = 4


def swapped(value, axis, apart):
    return lax.ppermute(value, axis, [(i, i ^ 1 << apart) for i in range(lax.axis_size(axis))])


def padded(value, sides, width):
    for axis, dim in sides:
        count, length = (lax.axis_size(axis), value.shape[dim])
        up = [(i, (i + 1) % count) for i in range(count - 1)]
        down = [(j, i) for i, j in up]
        last = lax.slice_in_dim(value, length - width, length, axis=dim)
        first = lax.slice_in_dim(value, 0, width, axis=dim)
        before = lax.ppermute(last, axis, up)
        after = lax.ppermute(first, axis, down)
        value = jnp.concatenate([before, value, after], axis=dim)
    return value


def butterfly(coeff, blocks):
    bits = lax.axis_size("wide").bit_length() - 1
    for level in range(LEVELS):
        partner = swapped(coeff, "wide", level % bits)
        summed = jnp.dot(blocks[level, 0], coeff, preferred_element_type=jnp.float32) + jnp.dot(
            blocks[level, 1], partner, preferred_element_type=jnp.float32
        )
        coeff = summed.astype(jnp.bfloat16)
    return coeff


def on_device(sources, order, near_cols, near_blocks, in_basis, transfer, out_basis):
    rows = sources.shape[0]
    rhs_cols = sources.shape[1]
    block_rows = near_blocks.shape[2]
    row_blocks = rows // block_rows
    local_ids = order % rows
    permuted = jnp.take(sources, local_ids, axis=0)
    term = jnp.dot(in_basis.T, permuted, preferred_element_type=jnp.float32)
    blocks = transfer[:, 0]
    coeff = lax.psum(term, "narrow").astype(jnp.bfloat16)
    coarse = butterfly(coeff, blocks)
    far = jnp.dot(out_basis, coarse, preferred_element_type=jnp.float32)
    extended = padded(permuted, (("narrow", 0),), REACH * block_rows)
    ext_blocks = extended.reshape(row_blocks + 2 * REACH, block_rows, rhs_cols)
    first_block = (
        lax.axis_index("wide") * lax.axis_size("narrow") + lax.axis_index("narrow")
    ) * row_blocks
    ext_ids = near_cols - first_block + REACH
    picked = jnp.take(ext_blocks, ext_ids, axis=0)
    near = jnp.einsum("reij,rejc->ric", near_blocks, picked, preferred_element_type=jnp.float32)
    return (far + near.reshape(rows, rhs_cols)).astype(jnp.bfloat16)


def solution(mesh):
    return jax.shard_map(
        on_device,
        mesh=mesh,
        in_specs=(
            P(("wide", "narrow"), None),
            P(("wide", "narrow")),
            P(("wide", "narrow"), None),
            P(("wide", "narrow"), None, None, None),
            P(("wide", "narrow"), None),
            P(None, "wide", None, None, None),
            P(("wide", "narrow"), None),
        ),
        out_specs=P(("wide", "narrow"), None),
        check_vma=False,
    )
```

profile of v0, /device:TPU:1, one launch (start us, length us, event | category | flops | bytes accessed | tf_op | source)
XLA Modules:
  0.0 104.9 jit_solution(15153493940416577841)
XLA Ops:
  0.0 0.0 copy-start
  0.0 0.9 compare_and_fusion
  0.9 0.7 broadcast_clamp_fusion
  1.6 0.0 copy-done
  1.6 9.2 %gather_fusion = bf16[2048,512]{1,0:T(8,128)(2,1)} fusion(bf16[2048,512]{1,0:T(8,128)(2,1)S(1)} %copy-done, s32[2048]{0:T(1024)S(1)} %broadcast_clamp_fusion), kind=kCustom, calls=%fused_computation | custom fusion | bytes 4202496 | tf_op jit(solution)/shard_map/jit(_take)/gather | solution.py:44
  10.8 0.0 copy-start.3
  10.8 1.9 %broadcast_select_fusion = bf16[2048,512]{1,0:T(8,128)(2,1)S(1)} fusion(bf16[2048,512]{1,0:T(8,128)(2,1)} %gather_fusion, pred[2048]{0:T(1024)(128)(4,1)S(1)} %compare_and_fusion), kind=kLoop, calls=%fused_computation.9 | loop fusion | flops 1048576 | bytes 4196352 | tf_op jit(solution)/shard_map/jit(_take)/select_n | solution.py:44
  12.7 0.0 copy-start.1
  12.7 1.3 %copy-done.1 = bf16[2048,512]{1,0:T(8,128)(2,1)} copy-done((bf16[2048,512]{1,0:T(8,128)(2,1)}, bf16[2048,512]{1,0:T(8,128)(2,1)S(1)}, u32[]{:S(2)}) %copy-start.1) | copy-done | bytes 2097176
  14.0 0.0 copy-done.3
  14.0 0.0 copy-start.4
  14.0 0.7 convolution_bitcast_fusion
  14.7 17.7 %all-reduce.1 = bf16[256,512]{0,1:T(8,128)(2,1)S(1)} all-reduce(f32[256,512]{0,1:T(8,128)S(1)} %convolution_bitcast_fusion), channel_id=1, replica_groups=mesh['wide'=64,'narrow'=4] {'narrow'}, use_global_device_ids=true, to_apply=%region_0.1 | all-reduce | flops 131072 | bytes 786432 | tf_op jit(solution)/shard_map/psum | solution.py:47
  32.4 0.0 copy-start.2
  32.5 0.9 collective-permute-start
  33.3 2.3 %fusion.15 = (bf16[512,512]{1,0:T(8,128)(2,1)}, bf16[512,512]{1,0:T(8,128)(2,1)}) fusion(bf16[2048,512]{1,0:T(8,128)(2,1)} %copy-done.1), kind=kLoop, calls=%fused_computation.42 | loop fusion | bytes 2097152 | tf_op jit(solution)/shard_map/slice | solution.py:19
  35.6 4.4 %collective-permute-start.4 = (bf16[512,512]{1,0:T(8,128)(2,1)}, bf16[512,512]{1,0:T(8,128)(2,1)}, u32[]{:S(2)}, u32[]{:S(2)}) collective-permute-start(bf16[512,512]{1,0:T(8,128)(2,1)} %get-tuple-element.7), channel_id=1, source_target_pairs={{0,1},{1,2},{2,3},{4,5},{5,6},{6,7},{8,9},{9,10},{10,11},{12,13},{... | collective-permute-start | bytes 1572872 | tf_op jit(solution)/shard_map/ppermute | solution.py:21
  40.0 1.9 %collective-permute-start.5 = (bf16[512,512]{1,0:T(8,128)(2,1)}, bf16[512,512]{1,0:T(8,128)(2,1)}, u32[]{:S(2)}, u32[]{:S(2)}) collective-permute-start(bf16[512,512]{1,0:T(8,128)(2,1)} %get-tuple-element.8), channel_id=1, source_target_pairs={{1,0},{2,1},{3,2},{5,4},{6,5},{7,6},{9,8},{10,9},{11,10},{13,12},{... | collective-permute-start | bytes 1572872 | tf_op jit(solution)/shard_map/ppermute | solution.py:22
  41.9 0.0 copy-done.4
  42.0 0.1 copy.13
  42.0 0.1 reshape.28
  42.1 1.2 %fusion.12 = f32[512,256]{1,0:T(8,128)S(1)} fusion(bf16[256,512]{0,1:T(8,128)(2,1)S(1)} %all-reduce.1, bf16[4,2,256,256]{3,2,1,0:T(8,128)(2,1)} %bitcast.58), kind=kOutput, calls=%fused_computation.30 | convolution fusion | flops 67108864 | bytes 917504 | tf_op jit(solution)/shard_map/dot_general | solution.py:31
  43.3 0.0 collective-permute-done
  43.3 1.2 %fusion.5 = bf16[512,256]{1,0:T(8,128)(2,1)S(1)} fusion(f32[512,256]{1,0:T(8,128)S(1)} %fusion.12, bf16[256,512]{0,1:T(8,128)(2,1)} %collective-permute-done, bf16[4,2,256,256]{3,2,1,0:T(8,128)(2,1)} %bitcast.59), kind=kOutput, calls=%fused_computation.15 | convolution fusion | flops 67371008 | bytes 1179648 | tf_op jit(solution)/shard_map/dot_general | solution.py:31
  44.5 2.5 %collective-permute-start.1 = (bf16[256,512]{0,1:T(8,128)(2,1)S(1)}, bf16[256,512]{0,1:T(8,128)(2,1)}, u32[]{:S(2)}, u32[]{:S(2)}) collective-permute-start(bf16[256,512]{0,1:T(8,128)(2,1)S(1)} %bitcast.67), channel_id=1, source_target_pairs={{0,8},{4,12},{8,0},{12,4},{16,24},{20,28},{24,16},{28,20},{32,40},... | collective-permute-start | bytes 786440 | tf_op jit(solution)/shard_map/ppermute | solution.py:11
  47.1 0.1 copy.12
  47.2 0.0 copy-done.2
  47.2 0.2 fusion.11
  47.4 6.4 %collective-permute-done.1 = bf16[256,512]{0,1:T(8,128)(2,1)} collective-permute-done((bf16[256,512]{0,1:T(8,128)(2,1)S(1)}, bf16[256,512]{0,1:T(8,128)(2,1)}, u32[]{:S(2)}, u32[]{:S(2)}) %collective-permute-start.1) | collective-permute-done | bytes 262176 | tf_op jit(solution)/shard_map/ppermute | solution.py:11
  53.9 1.2 %fusion.6 = bf16[512,256]{1,0:T(8,128)(2,1)S(1)} fusion(f32[512,256]{1,0:T(8,128)S(1)} %fusion.11, bf16[256,512]{0,1:T(8,128)(2,1)} %collective-permute-done.1, bf16[4,2,256,256]{3,2,1,0:T(8,128)(2,1)S(1)} %bitcast.63), kind=kOutput, calls=%fused_computation.16 | convolution fusion | flops 67371008 | bytes 1179648 | tf_op jit(solution)/shard_map/dot_general | solution.py:31
  55.1 3.1 %collective-permute-start.2 = (bf16[256,512]{0,1:T(8,128)(2,1)S(1)}, bf16[256,512]{0,1:T(8,128)(2,1)}, u32[]{:S(2)}, u32[]{:S(2)}) collective-permute-start(bf16[256,512]{0,1:T(8,128)(2,1)S(1)} %bitcast.66), channel_id=1, source_target_pairs={{0,16},{4,20},{8,24},{12,28},{16,0},{20,4},{24,8},{28,12},{32,48},... | collective-permute-start | bytes 786440 | tf_op jit(solution)/shard_map/ppermute | solution.py:11
  58.1 0.0 collective-permute-done.4
  58.1 0.0 collective-permute-done.5
  58.1 3.2 %pad_maximum_fusion = bf16[3072,512]{1,0:T(8,128)(2,1)} fusion(bf16[512,512]{1,0:T(8,128)(2,1)} %collective-permute-done.5, bf16[2048,512]{1,0:T(8,128)(2,1)} %copy-done.1, bf16[512,512]{1,0:T(8,128)(2,1)} %collective-permute-done.4), kind=kLoop, calls=%fused_computation.8 | loop fusion | flops 9437184 | bytes 6291456 | tf_op jit(solution)/shard_map/concatenate | solution.py:23
  61.3 10.2 %gather_fusion.1 = bf16[128,128,512]{2,1,0:T(8,128)(2,1)} fusion(bf16[24,128,512]{2,1,0:T(8,128)(2,1)} %bitcast.55, s32[1024]{0:T(1024)S(1)} %pad_clamp_fusion), kind=kCustom, calls=%fused_computation.1 | custom fusion | bytes 33554944 | tf_op jit(solution)/shard_map/jit(_take)/gather | solution.py:56
  71.5 0.2 fusion.10
  71.7 0.0 collective-permute-done.2
  71.7 1.2 %fusion.7 = bf16[512,256]{1,0:T(8,128)(2,1)S(1)} fusion(f32[512,256]{1,0:T(8,128)S(1)} %fusion.10, bf16[256,512]{0,1:T(8,128)(2,1)} %collective-permute-done.2, bf16[4,2,256,256]{3,2,1,0:T(8,128)(2,1)S(1)} %bitcast.65), kind=kOutput, calls=%fused_computation.17 | convolution fusion | flops 67371008 | bytes 1179648 | tf_op jit(solution)/shard_map/dot_general | solution.py:31
  73.0 4.4 %collective-permute-start.3 = (bf16[256,512]{0,1:T(8,128)(2,1)S(1)}, bf16[256,512]{0,1:T(8,128)(2,1)S(1)}, u32[]{:S(2)}, u32[]{:S(2)}) collective-permute-start(bf16[256,512]{0,1:T(8,128)(2,1)S(1)} %bitcast.68), channel_id=1, source_target_pairs={{0,32},{4,36},{8,40},{12,44},{16,48},{20,52},{24,56},{28,60},{32,0... | collective-permute-start | bytes 786440 | tf_op jit(solution)/shard_map/ppermute | solution.py:11
  77.3 12.3 %fusion = f32[16,512,128,1]{1,2,3,0:T(8,128)} fusion(bf16[16,8,128,128]{3,2,1,0:T(8,128)(2,1)} %param.10, bf16[16,8,128,512]{3,2,1,0:T(8,128)(2,1)} %bitcast.56, pred[16,8]{1,0:T(8,128)(4,1)S(1)} %copy.12), kind=kOutput, calls=%fused_computation.2 | convolution fusion | flops 2155872256 | bytes 25165952 | tf_op jit(solution)/shard_map/reij,rejc->ric/dot_general | solution.py:57
  89.6 5.4 %copy.17 = f32[2048,512]{0,1:T(8,128)} copy(f32[2048,512]{1,0:T(8,128)} %bitcast.57) | data formatting | bytes 8388608 | tf_op jit(solution)/shard_map/reshape | solution.py:58
  95.0 1.2 %fusion.9 = f32[512,256]{1,0:T(8,128)S(1)} fusion(bf16[512,256]{1,0:T(8,128)(2,1)S(1)} %fusion.7, bf16[4,2,256,256]{3,2,1,0:T(8,128)(2,1)} %bitcast.60), kind=kOutput, calls=%fused_computation.21 | convolution fusion | flops 67108864 | bytes 917504 | tf_op jit(solution)/shard_map/dot_general | solution.py:31
  96.2 0.0 collective-permute-done.3
  96.2 4.8 %fusion.4 = bf16[2048,512]{0,1:T(8,128)(2,1)} fusion(f32[2048,512]{0,1:T(8,128)} %copy.17, bf16[2048,256]{1,0:T(8,128)(2,1)} %param.13, f32[512,256]{1,0:T(8,128)S(1)} %fusion.9, bf16[256,512]{0,1:T(8,128)(2,1)S(1)} %collective-permute-done.3, bf16[4,2,256,256]{3,2,1,0:T(8,128)(2,1)} %bitcast.61), kind=kOutput, calls=%fused_computation.7 | convolution fusion | flops 606339072 | bytes 8257536 | tf_op jit(solution)/shard_map/dot_general | solution.py:49
  100.9 3.9 %copy.15 = bf16[2048,512]{1,0:T(8,128)(2,1)} copy(bf16[2048,512]{0,1:T(8,128)(2,1)} %fusion.4) | data formatting | bytes 4194304 | tf_op jit(solution)/shard_map/convert_element_type | solution.py:58
  (2 shorter events, 0.0 us)
Async XLA Ops:
  0.0 1.6 %copy-start = (bf16[2048,512]{1,0:T(8,128)(2,1)S(1)}, bf16[2048,512]{1,0:T(8,128)(2,1)}, u32[]{:S(2)}) copy-start(bf16[2048,512]{1,0:T(8,128)(2,1)} %param.7) | copy-start | bytes 6291460
  10.8 3.2 %copy-start.3 = (bf16[2048,256]{1,0:T(8,128)(2,1)S(1)}, bf16[2048,256]{1,0:T(8,128)(2,1)}, u32[]{:S(2)}) copy-start(bf16[2048,256]{1,0:T(8,128)(2,1)} %param.11) | copy-start | bytes 3145732
  12.7 1.3 %copy-start.1 = (bf16[2048,512]{1,0:T(8,128)(2,1)}, bf16[2048,512]{1,0:T(8,128)(2,1)S(1)}, u32[]{:S(2)}) copy-start(bf16[2048,512]{1,0:T(8,128)(2,1)S(1)} %broadcast_select_fusion) | copy-start | bytes 6291460
  14.0 27.9 %copy-start.4 = (s32[16,8]{0,1:T(8,128)S(1)}, s32[16,8]{0,1:T(8,128)}, u32[]{:S(2)}) copy-start(s32[16,8]{0,1:T(8,128)} %param.9) | copy-start | bytes 1540
  32.4 14.7 %copy-start.2 = (bf16[4,1,2,256,256]{4,3,2,1,0:T(8,128)(2,1)S(1)}, bf16[4,1,2,256,256]{4,3,2,1,0:T(8,128)(2,1)}, u32[]{:S(2)}) copy-start(bf16[4,1,2,256,256]{4,3,2,1,0:T(8,128)(2,1)} %param.12) | copy-start | bytes 3145732
  32.5 10.8 %collective-permute-start = (bf16[256,512]{0,1:T(8,128)(2,1)S(1)}, bf16[256,512]{0,1:T(8,128)(2,1)}, u32[]{:S(2)}, u32[]{:S(2)}) collective-permute-start(bf16[256,512]{0,1:T(8,128)(2,1)S(1)} %all-reduce.1), channel_id=1, source_target_pairs={{0,4},{4,0},{8,12},{12,8},{16,20},{20,16},{24,28},{28,24},{32,36},... | collective-permute-start | bytes 786440 | tf_op jit(solution)/shard_map/ppermute | solution.py:11
  35.6 22.5 %collective-permute-start.4 = (bf16[512,512]{1,0:T(8,128)(2,1)}, bf16[512,512]{1,0:T(8,128)(2,1)}, u32[]{:S(2)}, u32[]{:S(2)}) collective-permute-start(bf16[512,512]{1,0:T(8,128)(2,1)} %get-tuple-element.7), channel_id=1, source_target_pairs={{0,1},{1,2},{2,3},{4,5},{5,6},{6,7},{8,9},{9,10},{10,11},{12,13},{... | collective-permute-start | bytes 1572872 | tf_op jit(solution)/shard_map/ppermute | solution.py:21
  40.0 18.2 %collective-permute-start.5 = (bf16[512,512]{1,0:T(8,128)(2,1)}, bf16[512,512]{1,0:T(8,128)(2,1)}, u32[]{:S(2)}, u32[]{:S(2)}) collective-permute-start(bf16[512,512]{1,0:T(8,128)(2,1)} %get-tuple-element.8), channel_id=1, source_target_pairs={{1,0},{2,1},{3,2},{5,4},{6,5},{7,6},{9,8},{10,9},{11,10},{13,12},{... | collective-permute-start | bytes 1572872 | tf_op jit(solution)/shard_map/ppermute | solution.py:22
  44.5 9.3 %collective-permute-start.1 = (bf16[256,512]{0,1:T(8,128)(2,1)S(1)}, bf16[256,512]{0,1:T(8,128)(2,1)}, u32[]{:S(2)}, u32[]{:S(2)}) collective-permute-start(bf16[256,512]{0,1:T(8,128)(2,1)S(1)} %bitcast.67), channel_id=1, source_target_pairs={{0,8},{4,12},{8,0},{12,4},{16,24},{20,28},{24,16},{28,20},{32,40},... | collective-permute-start | bytes 786440 | tf_op jit(solution)/shard_map/ppermute | solution.py:11
  55.1 16.7 %collective-permute-start.2 = (bf16[256,512]{0,1:T(8,128)(2,1)S(1)}, bf16[256,512]{0,1:T(8,128)(2,1)}, u32[]{:S(2)}, u32[]{:S(2)}) collective-permute-start(bf16[256,512]{0,1:T(8,128)(2,1)S(1)} %bitcast.66), channel_id=1, source_target_pairs={{0,16},{4,20},{8,24},{12,28},{16,0},{20,4},{24,8},{28,12},{32,48},... | collective-permute-start | bytes 786440 | tf_op jit(solution)/shard_map/ppermute | solution.py:11
  73.0 23.2 %collective-permute-start.3 = (bf16[256,512]{0,1:T(8,128)(2,1)S(1)}, bf16[256,512]{0,1:T(8,128)(2,1)S(1)}, u32[]{:S(2)}, u32[]{:S(2)}) collective-permute-start(bf16[256,512]{0,1:T(8,128)(2,1)S(1)} %bitcast.68), channel_id=1, source_target_pairs={{0,32},{4,36},{8,40},{12,44},{16,48},{20,52},{24,56},{28,60},{32,0... | collective-permute-start | bytes 786440 | tf_op jit(solution)/shard_map/ppermute | solution.py:11
where the time goes:
time: 105 us
  local copies, waits for them, and re-layouts  32.6 us (31%)
  matrix products  24.3 us (23%)
  blocking collectives  17.7 us (17%)
  starting transfers between devices  17.1 us (16%)
  other arithmetic  6.6 us (6%)
  waiting for transfers between devices  6.46 us (6%)
    psum x1, blocking collectives, on_device(): coeff = lax.psum(term, 'narrow').astype(jnp.bfloat16)  17.7 us
    dot_general x1, matrix products, on_device(): jnp.einsum('reij,rejc->ric', near_blocks, picked, preferred_element_type=...  12.3 us
    ppermute x4, starting transfers between devices, swapped(): lax.ppermute(value, axis, [(i, i ^ 1 << apart) for i in range(lax.axis_si...  10.8 us
    gather x1, local copies, waits for them, and re-layouts, on_device(): picked = jnp.take(ext_blocks, ext_ids, axis=0)  10.2 us
    gather x1, local copies, waits for them, and re-layouts, on_device(): permuted = jnp.take(sources, local_ids, axis=0)  9.2 us
    ppermute x4, waiting for transfers between devices, swapped(): lax.ppermute(value, axis, [(i, i ^ 1 << apart) for i in range(lax.axis_si...  6.45 us
    reshape x1, local copies, waits for them, and re-layouts, on_device(): return (far + near.reshape(rows, rhs_cols)).astype(jnp.bfloat16)  5.38 us
    dot_general x1, matrix products, on_device(): far = jnp.dot(out_basis, coarse, preferred_element_type=jnp.float32)  4.77 us
  transfers between devices with their start and end apart: 6, of which 1 were waited for; matrix products, arithmetic and copies ran while one was open for 37% of the time, Pallas kernels for 0%

commit v1 on v0

v1 whole, which is shorter than its diff:
```python
import functools

import jax
import jax.numpy as jnp
from jax import lax
from jax.experimental import pallas as pl
from jax.experimental.pallas import tpu as pltpu
from jax.sharding import PartitionSpec as P

F32, BF16, I32 = jnp.float32, jnp.bfloat16, jnp.int32
MESH = pl.DeviceIdType.MESH
ROWS = 2048
RHS = 512
RANK = 256
BLOCK = 128
REACH = 4
NEAR = 8
BLOCKS_DEV = ROWS // BLOCK
OFFSETS = 2 * REACH + 1
CLUSTER_BLOCKS = 64
HALO = REACH * BLOCK
QUARTER = RHS // 4
GATHER_ROWS = 512
SCATTER_ROWS = 1024
VMEM, SMEM, DMA = pltpu.VMEM, pltpu.SMEM, pltpu.SemaphoreType.DMA


def flip(index, bit):
    return index + bit - 2 * bit * ((index // bit) % 2)


def dot(a, b):
    return jnp.dot(a, b, preferred_element_type=F32)


def tree_kernel(
    order_h, cols_h, sources_h, basis_h, blocks_h, transfer_h,
    coarse_o, near_o,
    order, cols, sources, basis, blocks, transfer,
    order_col, table_v, table_s, moved, permuted, part, part_b, core_in,
    z_out, z_in, c0, x_in, transfer_x, c2, h1_in, c3, h2_in, coarse,
    load, table_sem, send, recv, halo_send, halo_recv,
):
    w, n = lax.axis_index("wide"), lax.axis_index("narrow")
    first_row = (w * 4 + n) * ROWS
    quarter = flip(n, 2) * ((w // 8) % 2) + n * (1 - (w // 8) % 2)
    core = (w, flip(n, 1))
    zside = (w, flip(n, 2))
    cross = (w, flip(flip(n, 1), 2))
    x1, x2, x3 = (flip(w, 1), n), (flip(w, 2), n), (flip(flip(w, 1), 2), n)
    h1, h2 = (flip(w, 4), n), (flip(w, 8), flip(n, 2))

    loads = [
        pltpu.make_async_copy(a, b, load.at[i])
        for i, (a, b) in enumerate(
            (
                (order_h, order),
                (basis_h, basis),
                (sources_h, sources),
                (cols_h, cols),
                (transfer_h, transfer),
                (blocks_h, blocks),
            )
        )
    ]
    for one in loads:
        one.start()
    barrier = pltpu.get_barrier_semaphore()
    partners = (core, zside, cross, x1, x2, x3, h1, h2)
    for who in partners:
        pl.semaphore_signal(barrier, inc=1, device_id=who, device_id_type=MESH)

    def remote(src, dst, i, who):
        return pltpu.make_async_remote_copy(
            src_ref=src, dst_ref=dst, send_sem=send.at[i], recv_sem=recv.at[i],
            device_id=who, device_id_type=MESH,
        )

    loads[0].wait()
    loads[1].wait()

    def move(b, _):
        at = pl.multiple_of(b * SCATTER_ROWS, SCATTER_ROWS)
        ids = lax.broadcasted_iota(I32, (SCATTER_ROWS, BLOCK), 0) + (first_row + at)
        hot = jnp.concatenate(
            [jnp.where(ids == order[k : k + 1, :], 1.0, 0.0).astype(BF16) for k in range(BLOCKS_DEV)],
            axis=1,
        )
        moved[pl.ds(at, SCATTER_ROWS), :] = dot(hot, basis[...]).astype(BF16)
        return 0

    lax.fori_loop(0, ROWS // SCATTER_ROWS, move, 0)
    loads[4].wait()
    pl.semaphore_wait(barrier, len(partners))
    send_tx = remote(transfer.at[0], transfer_x, 0, x2)
    send_tx.start()

    loads[2].wait()
    term = lax.dot_general(
        moved[...], sources[...], (((0,), (0,)), ((), ())), preferred_element_type=F32
    )
    for k in range(4):
        piece = term[:, k * QUARTER : (k + 1) * QUARTER]
        part[k] = piece
        part_b[k] = piece.astype(BF16)
    q1, q2 = flip(quarter, 1), flip(quarter, 2)
    q3 = flip(q1, 2)
    send_c1 = remote(part_b.at[q3], core_in.at[1], 1, core)
    send_c0 = remote(part_b.at[q1], core_in.at[0], 2, core)
    send_c1.start()
    send_c0.start()

    turned = order[...].T
    for k in range(BLOCKS_DEV):
        order_col[k] = jnp.broadcast_to(turned[:, k : k + 1], (BLOCK, BLOCK))

    def gather(b, _):
        lanes = lax.broadcasted_iota(I32, (BLOCK, BLOCK), 1) + first_row
        rows = []
        for k in range(GATHER_ROWS // BLOCK):
            ids = order_col[b * (GATHER_ROWS // BLOCK) + k]
            rows.append(
                jnp.concatenate(
                    [jnp.where(lanes + c * BLOCK == ids, 1.0, 0.0).astype(BF16) for c in range(BLOCKS_DEV)],
                    axis=1,
                )
            )
        hot = jnp.concatenate(rows, axis=0)
        at = pl.multiple_of(b * GATHER_ROWS + HALO, HALO)
        permuted[pl.ds(at, GATHER_ROWS), :] = dot(hot, sources[...]).astype(BF16)
        return 0

    gather(3, 0)

    send_c1.wait_recv()
    z_out[...] = (part[q2] + core_in[1].astype(F32)).astype(BF16)
    send_z = remote(z_out, z_in, 3, zside)
    send_z.start()

    loads[3].wait()
    listed = cols[...]
    lane = lax.broadcasted_iota(I32, (NEAR, BLOCKS_DEV), 1)
    entry = lax.broadcasted_iota(I32, (NEAR, BLOCKS_DEV), 0)
    rank = jnp.zeros((NEAR, BLOCKS_DEV), I32)
    for e in range(NEAR - 1):
        same = jnp.where(listed == listed[e : e + 1, :], 1, 0)
        rank = rank + jnp.where(entry > e, same, 0)
    slot = listed - lane - (w * 4 + n) * BLOCKS_DEV + REACH
    slot = slot + jnp.where(listed == w * CLUSTER_BLOCKS, -rank, rank)
    for d in range(OFFSETS):
        table_v[d : d + 1, :BLOCKS_DEV] = jnp.sum(
            jnp.where(slot == d, entry + 1, 0), axis=0, keepdims=True
        )
    table_copy = pltpu.make_async_copy(table_v, table_s, table_sem)
    table_copy.start()

    gather(0, 0)

    send_c0.wait_recv()
    own = part[quarter] + core_in[0].astype(F32)
    send_z.wait_recv()
    c0[...] = (own + z_in[...].astype(F32)).astype(BF16)
    send_x = [remote(c0, x_in.at[i], 4 + i, who) for i, who in enumerate((x1, x2, x3))]
    for one in send_x:
        one.start()

    def halo_copy(up):
        if up:
            src, dst, who = permuted.at[pl.ds(ROWS, HALO)], permuted.at[pl.ds(0, HALO)], (n + 1) % 4
        else:
            src, dst, who = permuted.at[pl.ds(HALO, HALO)], permuted.at[pl.ds(ROWS + HALO, HALO)], (n + 3) % 4
        return pltpu.make_async_remote_copy(
            src_ref=src, dst_ref=dst, send_sem=halo_send.at[up], recv_sem=halo_recv.at[up],
            device_id=(w, who), device_id_type=MESH,
        )

    @pl.when(n < 3)
    def _():
        halo_copy(1).start()

    @pl.when(n > 0)
    def _():
        halo_copy(0).start()

    @pl.when(n == 0)
    def _():
        for k in range(REACH):
            permuted[k * BLOCK : (k + 1) * BLOCK, :] = permuted[HALO : HALO + BLOCK, :]

    @pl.when(n == 3)
    def _():
        for k in range(REACH):
            at = ROWS + HALO + k * BLOCK
            permuted[at : at + BLOCK, :] = permuted[ROWS + HALO - BLOCK : ROWS + HALO, :]

    lax.fori_loop(1, 3, gather, 0)
    table_copy.wait()
    loads[5].wait()

    def near_pair(p, _):
        def row(r):
            found = []
            for d in range(OFFSETS):
                at = table_s[d, r]
                block = blocks[r, jnp.maximum(at - 1, 0)]
                found.append(jnp.where(at > 0, block, jnp.zeros_like(block)))
            return found

        none = jnp.zeros((BLOCK, BLOCK), BF16)
        upper = jnp.concatenate(row(2 * p) + [none], axis=1)
        lower = jnp.concatenate([none] + row(2 * p + 1), axis=1)
        at = pl.multiple_of(p * 2 * BLOCK, 2 * BLOCK)
        near_o[pl.ds(at, 2 * BLOCK), :] = dot(
            jnp.concatenate([upper, lower], axis=0),
            permuted[pl.ds(at, (OFFSETS + 1) * BLOCK), :],
        )
        return 0

    lax.fori_loop(2, 5, near_pair, 0)

    for one in send_x:
        one.wait_recv()
    send_tx.wait_recv()
    c1 = (dot(transfer[0, 0], c0[...]) + dot(transfer[0, 1], x_in[0])).astype(BF16)
    c1x = (dot(transfer_x[0], x_in[1]) + dot(transfer_x[1], x_in[2])).astype(BF16)
    c2[...] = (dot(transfer[1, 0], c1) + dot(transfer[1, 1], c1x)).astype(BF16)
    send_h1 = remote(c2, h1_in, 7, h1)
    send_h1.start()

    lax.fori_loop(5, 6, near_pair, 0)

    @pl.when(n > 0)
    def _():
        halo_copy(1).wait_recv()

    @pl.when(n < 3)
    def _():
        halo_copy(0).wait_recv()

    lax.fori_loop(0, 2, near_pair, 0)

    send_h1.wait_recv()
    c3[...] = (dot(transfer[2, 0], c2[...]) + dot(transfer[2, 1], h1_in[...])).astype(BF16)
    send_h2 = remote(c3, h2_in, 8, h2)
    send_h2.start()

    lax.fori_loop(6, 8, near_pair, 0)

    send_h2.wait_recv()
    coarse[quarter] = (dot(transfer[3, 0], c3[...]) + dot(transfer[3, 1], h2_in[...])).astype(BF16)
    send_a = remote(coarse.at[quarter], coarse.at[quarter], 9, zside)
    send_b = remote(coarse.at[quarter], coarse.at[quarter], 10, core)
    send_a.start()
    send_b.start()
    remote(coarse.at[q2], coarse.at[q2], 9, zside).wait_recv()
    send_f = remote(coarse.at[q2], coarse.at[q2], 11, core)
    send_f.start()

    send_tx.wait_send()
    for one in (send_c0, send_c1, send_z, *send_x, send_h1, send_h2, send_a, send_b):
        one.wait_send()

    @pl.when(n < 3)
    def _():
        halo_copy(1).wait_send()

    @pl.when(n > 0)
    def _():
        halo_copy(0).wait_send()

    send_f.wait_send()
    remote(coarse.at[q1], coarse.at[q1], 10, core).wait_recv()
    remote(coarse.at[q3], coarse.at[q3], 11, core).wait_recv()
    coarse_o[...] = coarse[...]


def tree(order, cols, sources, basis, blocks, transfer):
    quarter = (RANK, QUARTER)
    scratch = [
        VMEM((BLOCKS_DEV, BLOCK), I32),
        VMEM((NEAR, BLOCKS_DEV), I32),
        VMEM((ROWS, RHS), BF16),
        VMEM((ROWS, RANK), BF16),
        VMEM((BLOCKS_DEV, NEAR, BLOCK, BLOCK), BF16),
        VMEM((4, 2, RANK, RANK), BF16),
        VMEM((BLOCKS_DEV, BLOCK, BLOCK), I32),
        VMEM((16, 128), I32),
        SMEM((16, 128), I32),
        VMEM((ROWS, RANK), BF16),
        VMEM((ROWS + 2 * HALO, RHS), BF16),
        VMEM((4, *quarter), F32),
        VMEM((4, *quarter), BF16),
        VMEM((2, *quarter), BF16),
        VMEM(quarter, BF16),
        VMEM(quarter, BF16),
        VMEM(quarter, BF16),
        VMEM((3, *quarter), BF16),
        VMEM((2, RANK, RANK), BF16),
        VMEM(quarter, BF16),
        VMEM(quarter, BF16),
        VMEM(quarter, BF16),
        VMEM(quarter, BF16),
        VMEM((4, *quarter), BF16),
        DMA((6,)),
        DMA,
        DMA((12,)),
        DMA((12,)),
        DMA((2,)),
        DMA((2,)),
    ]
    return pl.pallas_call(
        tree_kernel,
        out_shape=(VMEM((4, *quarter), BF16), VMEM((ROWS, RHS), F32)),
        in_specs=[pl.BlockSpec(memory_space=pltpu.HBM)] * 6,
        out_specs=[pl.BlockSpec(memory_space=VMEM)] * 2,
        scratch_shapes=scratch,
        compiler_params=pltpu.CompilerParams(
            collective_id=0, has_side_effects=True, vmem_limit_bytes=44 << 20
        ),
        name="tree",
    )(order, cols, sources, basis, blocks, transfer)


OUT_ROWS = 256


def far_kernel(basis_h, coarse, near, out_h, basis, out, load, store):
    count = ROWS // OUT_ROWS

    def rows(ref, i):
        return ref.at[pl.ds(i * OUT_ROWS, OUT_ROWS)]

    loads = [pltpu.make_async_copy(rows(basis_h, i), rows(basis, i), load.at[i]) for i in range(count)]
    stores = [pltpu.make_async_copy(rows(out, i), rows(out_h, i), store.at[i]) for i in range(count)]
    for one in loads:
        one.start()
    whole = jnp.concatenate([coarse[k] for k in range(4)], axis=1)
    for i in range(count):
        loads[i].wait()
        at = pl.ds(i * OUT_ROWS, OUT_ROWS)
        out[at, :] = (dot(basis[at, :], whole) + near[at, :]).astype(BF16)
        stores[i].start()
    for one in stores:
        one.wait()


def far(basis, coarse, near):
    count = ROWS // OUT_ROWS
    return pl.pallas_call(
        far_kernel,
        out_shape=jax.ShapeDtypeStruct((ROWS, RHS), BF16),
        in_specs=[
            pl.BlockSpec(memory_space=pl.ANY),
            pl.BlockSpec(memory_space=VMEM),
            pl.BlockSpec(memory_space=VMEM),
        ],
        out_specs=pl.BlockSpec(memory_space=pl.ANY),
        scratch_shapes=[
            VMEM((ROWS, RANK), BF16),
            VMEM((ROWS, RHS), BF16),
            DMA((count,)),
            DMA((count,)),
        ],
        compiler_params=pltpu.CompilerParams(vmem_limit_bytes=12 << 20),
        name="far",
    )(basis, coarse, near)


def on_device(sources, order, near_cols, near_blocks, in_basis, transfer, out_basis):
    given = (
        order.reshape(BLOCKS_DEV, BLOCK), near_cols.T, sources, in_basis, near_blocks, transfer[:, 0],
    )
    coarse, near = tree(*(pltpu.with_memory_space_constraint(x, pltpu.HBM) for x in given))
    return far(out_basis, coarse, near)


def solution(mesh):
    return jax.shard_map(
        on_device,
        mesh=mesh,
        in_specs=(
            P(("wide", "narrow"), None),
            P(("wide", "narrow")),
            P(("wide", "narrow"), None),
            P(("wide", "narrow"), None, None, None),
            P(("wide", "narrow"), None),
            P(None, "wide", None, None, None),
            P(("wide", "narrow"), None),
        ),
        out_specs=P(("wide", "narrow"), None),
        check_vma=False,
    )
```

time: 105 us -> 41.2 us (0.39)
  Pallas kernels: 0 us -> 41.1 us
  local copies, waits for them, and re-layouts: 32.6 us -> 0.01 us
  matrix products: 24.3 us -> 0 us
  blocking collectives: 17.7 us -> 0 us
  starting transfers between devices: 17.1 us -> 0 us
  other arithmetic: 6.6 us -> 0 us
  waiting for transfers between devices: 6.46 us -> 0 us
    pallas_call x0 -> x2, Pallas kernels: none -> 41.1 us  [the longest x1 37 us: tree(): pl.pallas_call(tree_kernel, out_shape=(VMEM((4, *quarter), BF16), VMEM((R...]
    dot_general x10 -> x0, matrix products: 24.3 us -> none  [the longest x1 12.3 us: on_device(): jnp.einsum('reij,rejc->ric', near_blocks, picked, preferred_element_type=...]
    gather x2 -> x0, local copies, waits for them, and re-layouts: 19.4 us -> none  [the longest x1 10.2 us: on_device(): picked = jnp.take(ext_blocks, ext_ids, axis=0)]
    psum x1 -> x0, blocking collectives: 17.7 us -> none  [on_device(): coeff = lax.psum(term, 'narrow').astype(jnp.bfloat16)]
    ppermute x6 -> x0, starting transfers between devices: 17.1 us -> none  [the longest x4 10.8 us: swapped(): lax.ppermute(value, axis, [(i, i ^ 1 << apart) for i in range(lax.axis_si...]
    ppermute x6 -> x0, waiting for transfers between devices: 6.46 us -> none  [the longest x4 6.45 us: swapped(): lax.ppermute(value, axis, [(i, i ^ 1 << apart) for i in range(lax.axis_si...]
    reshape x1 -> x0, local copies, waits for them, and re-layouts: 5.38 us -> none  [on_device(): return (far + near.reshape(rows, rhs_cols)).astype(jnp.bfloat16)]
    convert_element_type x1 -> x0, local copies, waits for them, and re-layouts: 3.92 us -> none  [on_device(): return (far + near.reshape(rows, rhs_cols)).astype(jnp.bfloat16)]
  transfers between devices with their start and end apart: 6 -> 0, of which waited for: 1 -> 0; matrix products, arithmetic and copies ran while one was open for 37% -> 0% of each run, Pallas kernels for 0% -> 0%
where the time goes in v1:
time: 41.2 us; the launch traced here: 41.1 us
  Pallas kernels  41.1 us (100%)
    pallas_call x1, Pallas kernels, tree(): pl.pallas_call(tree_kernel, out_shape=(VMEM((4, *quarter), BF16), VMEM((R...  37 us
    pallas_call x1, Pallas kernels, far(): pl.pallas_call(far_kernel, out_shape=jax.ShapeDtypeStruct((ROWS, RHS), BF...  4.09 us

profile of v1, /device:TPU:1, one launch (start us, length us, event | category | flops | bytes accessed | tf_op | source)
XLA Modules:
  0.0 41.1 jit_solution(8484487255126993879)
XLA Ops:
  0.0 0.0 copy-start
  0.0 37.0 %tree.1 = (bf16[4,256,128]{2,1,0:T(8,128)(2,1)S(1)}, f32[2048,512]{1,0:T(8,128)S(1)}) custom-call(s32[16,128]{1,0:T(8,128)} %bitcast.4, s32[8,16]{1,0:T(8,128)} %bitcast.5, bf16[2048,512]{1,0:T(8,128)(2,1)} %sources_h.1, bf16[2048,256]{1,0:T(8,128)(2,1)} %basis_h.2, bf16[16,8,128,128]{3,2,1,0:T(8,128)(2,1)} %blocks_h.1, bf16[4,2,256,256]{3,2,1,0:T(8,128)(2,1)} %bitcast.3), custom_call_target="tpu_custom_call" | custom-call | tf_op jit(solution)/shard_map/tree/pallas_call | solution.py:311
  37.0 0.0 copy-done
  37.0 4.1 %far.1 = bf16[2048,512]{1,0:T(8,128)(2,1)} custom-call(bf16[2048,256]{1,0:T(8,128)(2,1)S(1)} %copy-done, bf16[4,256,128]{2,1,0:T(8,128)(2,1)S(1)} %get-tuple-element.7.coarse, f32[2048,512]{1,0:T(8,128)S(1)} %get-tuple-element.8.near), custom_call_target="tpu_custom_call" | custom-call | tf_op jit(solution)/shard_map/far/pallas_call | solution.py:349
Async XLA Ops:
  0.0 37.0 %copy-start = (bf16[2048,256]{1,0:T(8,128)(2,1)S(1)}, bf16[2048,256]{1,0:T(8,128)(2,1)}, u32[]{:S(2)}) copy-start(bf16[2048,256]{1,0:T(8,128)(2,1)} %basis_h.3) | copy-start | bytes 3145732

commit v2 on v1

v2 whole, which is shorter than its diff:
```python
import functools

import jax
import jax.numpy as jnp
from jax import lax
from jax.experimental import pallas as pl
from jax.experimental.pallas import tpu as pltpu
from jax.sharding import PartitionSpec as P

F32, BF16, I32 = jnp.float32, jnp.bfloat16, jnp.int32
MESH = pl.DeviceIdType.MESH
ROWS = 2048
RHS = 512
RANK = 256
BLOCK = 128
REACH = 4
NEAR = 8
BLOCKS_DEV = ROWS // BLOCK
OFFSETS = 2 * REACH + 1
CLUSTER_BLOCKS = 64
HALO = REACH * BLOCK
QUARTER = RHS // 4
HALF = RHS // 2
PIECES = 2
PIECE = QUARTER // PIECES
GATHER_ROWS = 512
OUT_ROWS = 512
SCATTER_ROWS = 1024
VMEM, SMEM, DMA = pltpu.VMEM, pltpu.SMEM, pltpu.SemaphoreType.DMA


def flip(index, bit):
    return index + bit - 2 * bit * ((index // bit) % 2)


def dot(a, b):
    return jnp.dot(a, b, preferred_element_type=F32)


def dot_t(a, b):
    return lax.dot_general(a, b, (((1,), (1,)), ((), ())), preferred_element_type=F32)


def piece(p):
    return pl.ds(p * PIECE, PIECE)


def tree_kernel(
    order_h, cols_h, sources_h, basis_h, blocks_h, transfer_h, out_basis_h,
    other_o, near_o, own_o,
    order, cols, sources, basis, blocks, transfer, out_basis,
    order_col, table_v, table_s, moved, permuted, part, part_b, part_in,
    c0, x_in, transfer_x, c2, h1_in, c3, h2_in, coarse,
    load, table_sem, send, recv, halo_send, halo_recv,
):
    w, n = lax.axis_index("wide"), lax.axis_index("narrow")
    first_row = (w * 4 + n) * ROWS
    quarter = flip(n, 2) * ((w // 8) % 2) + n * (1 - (w // 8) % 2)
    core = (w, flip(n, 1))
    zside = (w, flip(n, 2))
    cross = (w, flip(flip(n, 1), 2))
    x1, x2, x3 = (flip(w, 1), n), (flip(w, 2), n), (flip(flip(w, 1), 2), n)
    h1, h2 = (flip(w, 4), n), (flip(w, 8), flip(n, 2))

    loads = [
        pltpu.make_async_copy(a, b, load.at[i])
        for i, (a, b) in enumerate(
            (
                (order_h, order),
                (basis_h, basis),
                (sources_h, sources),
                (transfer_h, transfer),
                (cols_h, cols),
                (blocks_h, blocks),
                (out_basis_h, out_basis),
            )
        )
    ]
    for one in loads[:2]:
        one.start()
    barrier = pltpu.get_barrier_semaphore()
    partners = (core, zside, cross, x1, x2, x3, h1, h2)
    for who in partners:
        pl.semaphore_signal(barrier, inc=1, device_id=who, device_id_type=MESH)

    def remote(src, dst, i, p, who):
        return pltpu.make_async_remote_copy(
            src_ref=src, dst_ref=dst, send_sem=send.at[i, p], recv_sem=recv.at[i, p],
            device_id=who, device_id_type=MESH,
        )

    loads[0].wait()
    loads[2].start()
    loads[1].wait()
    for one in loads[3:]:
        one.start()

    def move(b, _):
        at = pl.multiple_of(b * SCATTER_ROWS, SCATTER_ROWS)
        ids = lax.broadcasted_iota(I32, (SCATTER_ROWS, BLOCK), 0) + (first_row + at)
        hot = jnp.concatenate(
            [jnp.where(ids == order[k : k + 1, :], 1.0, 0.0).astype(BF16) for k in range(BLOCKS_DEV)],
            axis=1,
        )
        moved[pl.ds(at, SCATTER_ROWS), :] = dot(hot, basis[...]).astype(BF16)
        return 0

    lax.fori_loop(0, ROWS // SCATTER_ROWS, move, 0)
    loads[3].wait()
    pl.semaphore_wait(barrier, len(partners))
    side = n % 2
    send_tx = remote(transfer.at[0, side], transfer_x.at[side], 0, 0, x2)
    send_tx.start()

    loads[2].wait()
    half = quarter // 2
    q1, q2 = flip(quarter, 1), flip(quarter, 2)
    q3 = flip(q1, 2)

    def half_term(which):
        columns = sources[:, pl.ds(pl.multiple_of(which * HALF, HALF), HALF)]
        return lax.dot_general(
            columns, moved[...], (((0,), (0,)), ((), ())), preferred_element_type=F32
        )

    pair = (2, QUARTER, RANK)
    part_b[pl.ds(2 - 2 * half, 2)] = half_term(1 - half).astype(BF16).reshape(pair)
    send_c = [
        [
            remote(part_b.at[k, piece(p)], part_in.at[i, piece(p)], 1 + i, p, who)
            for i, (k, who) in enumerate(((q2, zside), (q3, cross), (q1, core)))
        ]
        for p in range(PIECES)
    ]
    for p in range(PIECES):
        for one in send_c[p][:2]:
            one.start()
    term = half_term(half).reshape(pair)
    part[...] = term
    part_b[pl.ds(2 * half, 2)] = term.astype(BF16)
    for p in range(PIECES):
        send_c[p][2].start()

    turned = order[...].T
    for k in range(BLOCKS_DEV):
        order_col[k] = jnp.broadcast_to(turned[:, k : k + 1], (BLOCK, BLOCK))

    def gather(b, _):
        lanes = lax.broadcasted_iota(I32, (BLOCK, BLOCK), 1) + first_row
        rows = []
        for k in range(GATHER_ROWS // BLOCK):
            ids = order_col[b * (GATHER_ROWS // BLOCK) + k]
            rows.append(
                jnp.concatenate(
                    [jnp.where(lanes + c * BLOCK == ids, 1.0, 0.0).astype(BF16) for c in range(BLOCKS_DEV)],
                    axis=1,
                )
            )
        hot = jnp.concatenate(rows, axis=0)
        at = pl.multiple_of(b * GATHER_ROWS + HALO, HALO)
        permuted[pl.ds(at, GATHER_ROWS), :] = dot(hot, sources[...]).astype(BF16)
        return 0

    gather(3, 0)

    loads[4].wait()
    listed = cols[...]
    lane = lax.broadcasted_iota(I32, (NEAR, BLOCKS_DEV), 1)
    entry = lax.broadcasted_iota(I32, (NEAR, BLOCKS_DEV), 0)
    rank = jnp.zeros((NEAR, BLOCKS_DEV), I32)
    for e in range(NEAR - 1):
        same = jnp.where(listed == listed[e : e + 1, :], 1, 0)
        rank = rank + jnp.where(entry > e, same, 0)
    slot = listed - lane - (w * 4 + n) * BLOCKS_DEV + REACH
    slot = slot + jnp.where(listed == w * CLUSTER_BLOCKS, -rank, rank)
    for d in range(OFFSETS):
        table_v[d : d + 1, :BLOCKS_DEV] = jnp.sum(
            jnp.where(slot == d, entry + 1, 0), axis=0, keepdims=True
        )
    table_copy = pltpu.make_async_copy(table_v, table_s, table_sem)
    table_copy.start()

    gather(0, 0)

    send_x = []
    for p in range(PIECES):
        for one in send_c[p]:
            one.wait_recv()
        own = part[quarter % 2, piece(p), :]
        for i in range(3):
            own = own + part_in[i, piece(p), :].astype(F32)
        c0[piece(p), :] = own.astype(BF16)
        send_x.append(
            [
                remote(c0.at[piece(p)], x_in.at[i, piece(p)], 4 + i, p, who)
                for i, who in ((1, x2), (0, x1), (2, x3))
            ]
        )
        for one in send_x[p]:
            one.start()

    def halo_copy(up):
        if up:
            src, dst, who = permuted.at[pl.ds(ROWS, HALO)], permuted.at[pl.ds(0, HALO)], (n + 1) % 4
        else:
            src, dst, who = permuted.at[pl.ds(HALO, HALO)], permuted.at[pl.ds(ROWS + HALO, HALO)], (n + 3) % 4
        return pltpu.make_async_remote_copy(
            src_ref=src, dst_ref=dst, send_sem=halo_send.at[up], recv_sem=halo_recv.at[up],
            device_id=(w, who), device_id_type=MESH,
        )

    @pl.when(n < 3)
    def _():
        halo_copy(1).start()

    @pl.when(n > 0)
    def _():
        halo_copy(0).start()

    @pl.when(n == 0)
    def _():
        for k in range(REACH):
            permuted[k * BLOCK : (k + 1) * BLOCK, :] = permuted[HALO : HALO + BLOCK, :]

    @pl.when(n == 3)
    def _():
        for k in range(REACH):
            at = ROWS + HALO + k * BLOCK
            permuted[at : at + BLOCK, :] = permuted[ROWS + HALO - BLOCK : ROWS + HALO, :]

    gather(1, 0)
    send_tx.wait_recv()
    pass_tx = remote(transfer_x.at[side], transfer_x.at[side], 0, 1, core)
    pass_tx.start()
    gather(2, 0)
    table_copy.wait()
    loads[5].wait()

    def near_pair(p, _):
        def row(r):
            found = []
            for d in range(OFFSETS):
                at = table_s[d, r]
                block = blocks[r, jnp.maximum(at - 1, 0)]
                found.append(jnp.where(at > 0, block, jnp.zeros_like(block)))
            return found

        none = jnp.zeros((BLOCK, BLOCK), BF16)
        upper = jnp.concatenate(row(2 * p) + [none], axis=1)
        lower = jnp.concatenate([none] + row(2 * p + 1), axis=1)
        at = pl.multiple_of(p * 2 * BLOCK, 2 * BLOCK)
        found = dot(
            jnp.concatenate([upper, lower], axis=0),
            permuted[pl.ds(at, (OFFSETS + 1) * BLOCK), :],
        )
        near_o[0, pl.ds(at, 2 * BLOCK), :] = found[:, :HALF]
        near_o[1, pl.ds(at, 2 * BLOCK), :] = found[:, HALF:]
        return 0

    lax.fori_loop(2, 3, near_pair, 0)

    remote(transfer_x.at[1 - side], transfer_x.at[1 - side], 0, 1, core).wait_recv()
    send_h1 = []
    for p in range(PIECES):
        for one in send_x[p]:
            one.wait_recv()
        c1 = dot_t(c0[piece(p), :], transfer[0, 0]) + dot_t(x_in[0, piece(p), :], transfer[0, 1])
        c1x = dot_t(x_in[1, piece(p), :], transfer_x[0]) + dot_t(x_in[2, piece(p), :], transfer_x[1])
        c2[piece(p), :] = (
            dot_t(c1.astype(BF16), transfer[1, 0]) + dot_t(c1x.astype(BF16), transfer[1, 1])
        ).astype(BF16)
        send_h1.append(remote(c2.at[piece(p)], h1_in.at[piece(p)], 7, p, h1))
        send_h1[p].start()

    lax.fori_loop(3, 6, near_pair, 0)

    @pl.when(n > 0)
    def _():
        halo_copy(1).wait_recv()

    @pl.when(n < 3)
    def _():
        halo_copy(0).wait_recv()

    lax.fori_loop(0, 1, near_pair, 0)

    send_h2 = []
    for p in range(PIECES):
        send_h1[p].wait_recv()
        c3[piece(p), :] = (
            dot_t(c2[piece(p), :], transfer[2, 0]) + dot_t(h1_in[piece(p), :], transfer[2, 1])
        ).astype(BF16)
        send_h2.append(remote(c3.at[piece(p)], h2_in.at[piece(p)], 8, p, h2))
        send_h2[p].start()

    lax.fori_loop(1, 2, near_pair, 0)
    lax.fori_loop(6, 8, near_pair, 0)
    loads[6].wait()

    def share(i, k, p, who):
        return remote(coarse.at[k, piece(p)], coarse.at[k, piece(p)], 9 + i, p, who)

    send_q = []
    for p in range(PIECES):
        send_h2[p].wait_recv()
        coarse[quarter, piece(p), :] = (
            dot_t(c3[piece(p), :], transfer[3, 0]) + dot_t(h2_in[piece(p), :], transfer[3, 1])
        ).astype(BF16)
        send_q += [share(i, quarter, p, who) for i, who in enumerate((zside, cross, core))]
        for one in send_q[-3:]:
            one.start()
    for p in range(PIECES):
        share(2, q1, p, core).wait_recv()

    held = coarse[pl.ds(2 * half, 2)].reshape(HALF, RANK)

    def far_rows(b, _):
        at = pl.ds(pl.multiple_of(b * OUT_ROWS, OUT_ROWS), OUT_ROWS)
        own_o[at, :] = (dot_t(out_basis[at, :], held) + near_o[half, at, :]).astype(BF16)
        return 0

    lax.fori_loop(0, ROWS // OUT_ROWS, far_rows, 0)

    send_tx.wait_send()
    pass_tx.wait_send()
    for one in (*send_c[0], *send_c[1], *send_x[0], *send_x[1], *send_h1, *send_h2, *send_q):
        one.wait_send()

    @pl.when(n < 3)
    def _():
        halo_copy(1).wait_send()

    @pl.when(n > 0)
    def _():
        halo_copy(0).wait_send()

    for p in range(PIECES):
        share(0, q2, p, zside).wait_recv()
        share(1, q3, p, cross).wait_recv()
    other_o[...] = coarse[pl.ds(2 - 2 * half, 2)].reshape(HALF, RANK)


def tree(order, cols, sources, basis, blocks, transfer, out_basis):
    quarter = (QUARTER, RANK)
    scratch = [
        VMEM((BLOCKS_DEV, BLOCK), I32),
        VMEM((NEAR, BLOCKS_DEV), I32),
        VMEM((ROWS, RHS), BF16),
        VMEM((ROWS, RANK), BF16),
        VMEM((BLOCKS_DEV, NEAR, BLOCK, BLOCK), BF16),
        VMEM((4, 2, RANK, RANK), BF16),
        VMEM((ROWS, RANK), BF16),
        VMEM((BLOCKS_DEV, BLOCK, BLOCK), I32),
        VMEM((16, 128), I32),
        SMEM((16, 128), I32),
        VMEM((ROWS, RANK), BF16),
        VMEM((ROWS + 2 * HALO, RHS), BF16),
        VMEM((2, *quarter), F32),
        VMEM((4, *quarter), BF16),
        VMEM((3, *quarter), BF16),
        VMEM(quarter, BF16),
        VMEM((3, *quarter), BF16),
        VMEM((2, RANK, RANK), BF16),
        VMEM(quarter, BF16),
        VMEM(quarter, BF16),
        VMEM(quarter, BF16),
        VMEM(quarter, BF16),
        VMEM((4, *quarter), BF16),
        DMA((7,)),
        DMA,
        DMA((12, PIECES)),
        DMA((12, PIECES)),
        DMA((2,)),
        DMA((2,)),
    ]
    return pl.pallas_call(
        tree_kernel,
        out_shape=(
            VMEM((HALF, RANK), BF16),
            VMEM((2, ROWS, HALF), F32),
            VMEM((ROWS, HALF), BF16),
        ),
        in_specs=[pl.BlockSpec(memory_space=pltpu.HBM)] * 7,
        out_specs=[pl.BlockSpec(memory_space=VMEM)] * 3,
        scratch_shapes=scratch,
        compiler_params=pltpu.CompilerParams(
            collective_id=0, has_side_effects=True, vmem_limit_bytes=44 << 20
        ),
        name="tree",
    )(order, cols, sources, basis, blocks, transfer, out_basis)


def far_kernel(basis, other, near, own, out_h, out, own_sem, store):
    count = ROWS // OUT_ROWS
    w, n = lax.axis_index("wide"), lax.axis_index("narrow")
    half = (flip(n, 2) * ((w // 8) % 2) + n * (1 - (w // 8) % 2)) // 2

    def columns(which):
        return pl.ds(pl.multiple_of(which * HALF, HALF), HALF)

    send_own = pltpu.make_async_copy(own, out_h.at[:, columns(half)], own_sem)
    send_own.start()
    stores = []
    for i in range(count):
        at = pl.ds(i * OUT_ROWS, OUT_ROWS)
        out[at, :] = (dot_t(basis[at, :], other[...]) + near[1 - half, at, :]).astype(BF16)
        stores.append(
            pltpu.make_async_copy(out.at[at], out_h.at[at, columns(1 - half)], store.at[i])
        )
        stores[-1].start()
    for one in stores:
        one.wait()
    send_own.wait()


def far(basis, other, near, own):
    return pl.pallas_call(
        far_kernel,
        out_shape=jax.ShapeDtypeStruct((ROWS, RHS), BF16),
        in_specs=[pl.BlockSpec(memory_space=VMEM)] * 4,
        out_specs=pl.BlockSpec(memory_space=pl.ANY),
        scratch_shapes=[VMEM((ROWS, HALF), BF16), DMA, DMA((ROWS // OUT_ROWS,))],
        compiler_params=pltpu.CompilerParams(vmem_limit_bytes=6 << 20),
        name="far",
    )(basis, other, near, own)


def on_device(sources, order, near_cols, near_blocks, in_basis, transfer, out_basis):
    given = (
        order.reshape(BLOCKS_DEV, BLOCK), near_cols.T, sources, in_basis, near_blocks, transfer[:, 0],
        out_basis,
    )
    other, near, own = tree(*(pltpu.with_memory_space_constraint(x, pltpu.HBM) for x in given))
    return far(out_basis, other, near, own)


def solution(mesh):
    return jax.shard_map(
        on_device,
        mesh=mesh,
        in_specs=(
            P(("wide", "narrow"), None),
            P(("wide", "narrow")),
            P(("wide", "narrow"), None),
            P(("wide", "narrow"), None, None, None),
            P(("wide", "narrow"), None),
            P(None, "wide", None, None, None),
            P(("wide", "narrow"), None),
        ),
        out_specs=P(("wide", "narrow"), None),
        check_vma=False,
    )
```

time: 41.2 us -> 35.4 us (0.86)
  Pallas kernels: 41.1 us -> 35.3 us
    pallas_call x1, Pallas kernels: 37 us -> 33.8 us  [tree(): pl.pallas_call(tree_kernel, out_shape=(VMEM((HALF, RANK), BF16), VMEM((2,...]
    pallas_call x1, Pallas kernels: 4.09 us -> 1.51 us  [far(): pl.pallas_call(far_kernel, out_shape=jax.ShapeDtypeStruct((ROWS, RHS), BF...]
where the time goes in v2:
time: 35.4 us; the launch traced here: 35.3 us
  Pallas kernels  35.3 us (100%)
    pallas_call x1, Pallas kernels, tree(): pl.pallas_call(tree_kernel, out_shape=(VMEM((HALF, RANK), BF16), VMEM((2,...  33.8 us
    pallas_call x1, Pallas kernels, far(): pl.pallas_call(far_kernel, out_shape=jax.ShapeDtypeStruct((ROWS, RHS), BF...  1.51 us

profile of v2, /device:TPU:1, one launch (start us, length us, event | category | flops | bytes accessed | tf_op | source)
XLA Modules:
  0.0 35.3 jit_solution(2498445488164799736)
XLA Ops:
  0.0 0.0 copy-start
  0.0 33.8 %tree.1 = (bf16[256,256]{1,0:T(8,128)(2,1)S(1)}, f32[2,2048,256]{2,1,0:T(8,128)S(1)}, bf16[2048,256]{1,0:T(8,128)(2,1)S(1)}) custom-call(s32[16,128]{1,0:T(8,128)} %bitcast.4, s32[8,16]{1,0:T(8,128)} %bitcast.5, bf16[2048,512]{1,0:T(8,128)(2,1)} %sources_h.1, bf16[2048,256]{1,0:T(8,128)(2,1)} %basis_h.1, bf16[16,8,128,128]{3,2,1,0:T(8,128)(2,1)} %blocks_h.1, ...), custom_call_target="tpu_custom_call" | custom-call | tf_op jit(solution)/shard_map/tree/pallas_call | solution.py:376
  33.8 0.0 copy-done
  33.8 1.5 %far.1 = bf16[2048,512]{1,0:T(8,128)(2,1)} custom-call(bf16[2048,256]{1,0:T(8,128)(2,1)S(1)} %copy-done, bf16[256,256]{1,0:T(8,128)(2,1)S(1)} %get-tuple-element.8.other, f32[2,2048,256]{2,1,0:T(8,128)S(1)} %get-tuple-element.9.near, bf16[2048,256]{1,0:T(8,128)(2,1)S(1)} %get-tuple-element.10.own), custom_call_target="tpu_custom_call" | custom-call | tf_op jit(solution)/shard_map/far/pallas_call | solution.py:417
Async XLA Ops:
  0.0 33.8 %copy-start = (bf16[2048,256]{1,0:T(8,128)(2,1)S(1)}, bf16[2048,256]{1,0:T(8,128)(2,1)}, u32[]{:S(2)}) copy-start(bf16[2048,256]{1,0:T(8,128)(2,1)} %basis.1) | copy-start | bytes 3145732

commit v3 on v2

--- a/solution.py
+++ b/solution.py
@@ -21,10 +21,11 @@
 HALO = REACH * BLOCK
 QUARTER = RHS // 4
 HALF = RHS // 2
-PIECES = 2
+PIECES = 4
 PIECE = QUARTER // PIECES
 GATHER_ROWS = 512
 OUT_ROWS = 512
+LAST_ROWS = 256
 SCATTER_ROWS = 1024
 VMEM, SMEM, DMA = pltpu.VMEM, pltpu.SMEM, pltpu.SemaphoreType.DMA
 
@@ -41,14 +42,20 @@
     return lax.dot_general(a, b, (((1,), (1,)), ((), ())), preferred_element_type=F32)
 
 
+def level(own, partner, pair):
+    return dot_t(
+        jnp.concatenate([own, partner], axis=1), jnp.concatenate([pair[0], pair[1]], axis=1)
+    ).astype(BF16)
+
+
 def piece(p):
     return pl.ds(p * PIECE, PIECE)
 
 
 def tree_kernel(
     order_h, cols_h, sources_h, basis_h, blocks_h, transfer_h, out_basis_h,
-    other_o, near_o, own_o,
-    order, cols, sources, basis, blocks, transfer, out_basis,
+    other_o, near_o, own_o, out_basis,
+    order, cols, sources, basis, blocks, transfer,
     order_col, table_v, table_s, moved, permuted, part, part_b, part_in,
     c0, x_in, transfer_x, c2, h1_in, c3, h2_in, coarse,
     load, table_sem, send, recv, halo_send, halo_recv,
@@ -91,6 +98,9 @@
 
     loads[0].wait()
     loads[2].start()
+    turned = order[...].T
+    for k in range(BLOCKS_DEV):
+        order_col[k] = jnp.broadcast_to(turned[:, k : k + 1], (BLOCK, BLOCK))
     loads[1].wait()
     for one in loads[3:]:
         one.start()
@@ -140,10 +150,6 @@
     part_b[pl.ds(2 * half, 2)] = term.astype(BF16)
     for p in range(PIECES):
         send_c[p][2].start()
-
-    turned = order[...].T
-    for k in range(BLOCKS_DEV):
-        order_col[k] = jnp.broadcast_to(turned[:, k : k + 1], (BLOCK, BLOCK))
 
     def gather(b, _):
         lanes = lax.broadcasted_iota(I32, (BLOCK, BLOCK), 1) + first_row
@@ -161,7 +167,26 @@
         permuted[pl.ds(at, GATHER_ROWS), :] = dot(hot, sources[...]).astype(BF16)
         return 0
 
-    gather(3, 0)
+    first = 3 - 3 * (n // 2)
+    gather(first, 0)
+
+    def halo_copy(up):
+        if up:
+            src, dst, who = permuted.at[pl.ds(ROWS, HALO)], permuted.at[pl.ds(0, HALO)], (n + 1) % 4
+        else:
+            src, dst, who = permuted.at[pl.ds(HALO, HALO)], permuted.at[pl.ds(ROWS + HALO, HALO)], (n + 3) % 4
+        return pltpu.make_async_remote_copy(
+            src_ref=src, dst_ref=dst, send_sem=halo_send.at[up], recv_sem=halo_recv.at[up],
+            device_id=(w, who), device_id_type=MESH,
+        )
+
+    @pl.when(n < 2)
+    def _():
+        halo_copy(1).start()
+
+    @pl.when(n >= 2)
+    def _():
+        halo_copy(0).start()
 
     loads[4].wait()
     listed = cols[...]
@@ -180,8 +205,6 @@
     table_copy = pltpu.make_async_copy(table_v, table_s, table_sem)
     table_copy.start()
 
-    gather(0, 0)
-
     send_x = []
     for p in range(PIECES):
         for one in send_c[p]:
@@ -199,21 +222,13 @@
         for one in send_x[p]:
             one.start()
 
-    def halo_copy(up):
-        if up:
-            src, dst, who = permuted.at[pl.ds(ROWS, HALO)], permuted.at[pl.ds(0, HALO)], (n + 1) % 4
-        else:
-            src, dst, who = permuted.at[pl.ds(HALO, HALO)], permuted.at[pl.ds(ROWS + HALO, HALO)], (n + 3) % 4
-        return pltpu.make_async_remote_copy(
-            src_ref=src, dst_ref=dst, send_sem=halo_send.at[up], recv_sem=halo_recv.at[up],
-            device_id=(w, who), device_id_type=MESH,
-        )
-
-    @pl.when(n < 3)
+    gather(3 - first, 0)
+
+    @pl.when(n == 2)
     def _():
         halo_copy(1).start()
 
-    @pl.when(n > 0)
+    @pl.when(n == 1)
     def _():
         halo_copy(0).start()
 
@@ -228,11 +243,10 @@
             at = ROWS + HALO + k * BLOCK
             permuted[at : at + BLOCK, :] = permuted[ROWS + HALO - BLOCK : ROWS + HALO, :]
 
-    gather(1, 0)
     send_tx.wait_recv()
     pass_tx = remote(transfer_x.at[side], transfer_x.at[side], 0, 1, core)
     pass_tx.start()
-    gather(2, 0)
+    gather(1, 0)
     table_copy.wait()
     loads[5].wait()
 
@@ -257,43 +271,38 @@
         near_o[1, pl.ds(at, 2 * BLOCK), :] = found[:, HALF:]
         return 0
 
-    lax.fori_loop(2, 3, near_pair, 0)
-
     remote(transfer_x.at[1 - side], transfer_x.at[1 - side], 0, 1, core).wait_recv()
     send_h1 = []
     for p in range(PIECES):
         for one in send_x[p]:
             one.wait_recv()
-        c1 = dot_t(c0[piece(p), :], transfer[0, 0]) + dot_t(x_in[0, piece(p), :], transfer[0, 1])
-        c1x = dot_t(x_in[1, piece(p), :], transfer_x[0]) + dot_t(x_in[2, piece(p), :], transfer_x[1])
-        c2[piece(p), :] = (
-            dot_t(c1.astype(BF16), transfer[1, 0]) + dot_t(c1x.astype(BF16), transfer[1, 1])
-        ).astype(BF16)
+        c1 = level(c0[piece(p), :], x_in[0, piece(p), :], transfer[0])
+        c1x = level(x_in[1, piece(p), :], x_in[2, piece(p), :], transfer_x[...])
+        c2[piece(p), :] = level(c1, c1x, transfer[1])
         send_h1.append(remote(c2.at[piece(p)], h1_in.at[piece(p)], 7, p, h1))
         send_h1[p].start()
 
-    lax.fori_loop(3, 6, near_pair, 0)
-
-    @pl.when(n > 0)
-    def _():
-        halo_copy(1).wait_recv()
-
-    @pl.when(n < 3)
-    def _():
-        halo_copy(0).wait_recv()
-
-    lax.fori_loop(0, 1, near_pair, 0)
+    gather(2, 0)
+    lax.fori_loop(2, 5, near_pair, 0)
 
     send_h2 = []
     for p in range(PIECES):
         send_h1[p].wait_recv()
-        c3[piece(p), :] = (
-            dot_t(c2[piece(p), :], transfer[2, 0]) + dot_t(h1_in[piece(p), :], transfer[2, 1])
-        ).astype(BF16)
+        c3[piece(p), :] = level(c2[piece(p), :], h1_in[piece(p), :], transfer[2])
         send_h2.append(remote(c3.at[piece(p)], h2_in.at[piece(p)], 8, p, h2))
         send_h2[p].start()
 
-    lax.fori_loop(1, 2, near_pair, 0)
+    lax.fori_loop(5, 6, near_pair, 0)
+
+    @pl.when(n > 0)
+    def _():
+        halo_copy(1).wait_recv()
+
+    @pl.when(n < 3)
+    def _():
+        halo_copy(0).wait_recv()
+
+    lax.fori_loop(0, 2, near_pair, 0)
     lax.fori_loop(6, 8, near_pair, 0)
     loads[6].wait()
 
@@ -303,9 +312,7 @@
     send_q = []
     for p in range(PIECES):
         send_h2[p].wait_recv()
-        coarse[quarter, piece(p), :] = (
-            dot_t(c3[piece(p), :], transfer[3, 0]) + dot_t(h2_in[piece(p), :], transfer[3, 1])
-        ).astype(BF16)
+        coarse[quarter, piece(p), :] = level(c3[piece(p), :], h2_in[piece(p), :], transfer[3])
         send_q += [share(i, quarter, p, who) for i, who in enumerate((zside, cross, core))]
         for one in send_q[-3:]:
             one.start()
@@ -323,7 +330,7 @@
 
     send_tx.wait_send()
     pass_tx.wait_send()
-    for one in (*send_c[0], *send_c[1], *send_x[0], *send_x[1], *send_h1, *send_h2, *send_q):
+    for one in (*sum(send_c, []), *sum(send_x, []), *send_h1, *send_h2, *send_q):
         one.wait_send()
 
     @pl.when(n < 3)
@@ -349,7 +356,6 @@
         VMEM((ROWS, RANK), BF16),
         VMEM((BLOCKS_DEV, NEAR, BLOCK, BLOCK), BF16),
         VMEM((4, 2, RANK, RANK), BF16),
-        VMEM((ROWS, RANK), BF16),
         VMEM((BLOCKS_DEV, BLOCK, BLOCK), I32),
         VMEM((16, 128), I32),
         SMEM((16, 128), I32),
@@ -379,9 +385,10 @@
             VMEM((HALF, RANK), BF16),
             VMEM((2, ROWS, HALF), F32),
             VMEM((ROWS, HALF), BF16),
+            VMEM((ROWS, RANK), BF16),
         ),
         in_specs=[pl.BlockSpec(memory_space=pltpu.HBM)] * 7,
-        out_specs=[pl.BlockSpec(memory_space=VMEM)] * 3,
+        out_specs=[pl.BlockSpec(memory_space=VMEM)] * 4,
         scratch_shapes=scratch,
         compiler_params=pltpu.CompilerParams(
             collective_id=0, has_side_effects=True, vmem_limit_bytes=44 << 20
@@ -391,7 +398,7 @@
 
 
 def far_kernel(basis, other, near, own, out_h, out, own_sem, store):
-    count = ROWS // OUT_ROWS
+    count = ROWS // LAST_ROWS
     w, n = lax.axis_index("wide"), lax.axis_index("narrow")
     half = (flip(n, 2) * ((w // 8) % 2) + n * (1 - (w // 8) % 2)) // 2
 
@@ -402,7 +409,7 @@
     send_own.start()
     stores = []
     for i in range(count):
-        at = pl.ds(i * OUT_ROWS, OUT_ROWS)
+        at = pl.ds(i * LAST_ROWS, LAST_ROWS)
         out[at, :] = (dot_t(basis[at, :], other[...]) + near[1 - half, at, :]).astype(BF16)
         stores.append(
             pltpu.make_async_copy(out.at[at], out_h.at[at, columns(1 - half)], store.at[i])
@@ -419,7 +426,7 @@
         out_shape=jax.ShapeDtypeStruct((ROWS, RHS), BF16),
         in_specs=[pl.BlockSpec(memory_space=VMEM)] * 4,
         out_specs=pl.BlockSpec(memory_space=pl.ANY),
-        scratch_shapes=[VMEM((ROWS, HALF), BF16), DMA, DMA((ROWS // OUT_ROWS,))],
+        scratch_shapes=[VMEM((ROWS, HALF), BF16), DMA, DMA((ROWS // LAST_ROWS,))],
         compiler_params=pltpu.CompilerParams(vmem_limit_bytes=6 << 20),
         name="far",
     )(basis, other, near, own)
@@ -430,8 +437,8 @@
         order.reshape(BLOCKS_DEV, BLOCK), near_cols.T, sources, in_basis, near_blocks, transfer[:, 0],
         out_basis,
     )
-    other, near, own = tree(*(pltpu.with_memory_space_constraint(x, pltpu.HBM) for x in given))
-    return far(out_basis, other, near, own)
+    other, near, own, basis = tree(*(pltpu.with_memory_space_constraint(x, pltpu.HBM) for x in given))
+    return far(basis, other, near, own)
 
 
 def solution(mesh):

time: 35.4 us -> 34.2 us (0.966)
  Pallas kernels: 35.3 us -> 34 us
    pallas_call x1, Pallas kernels: 33.8 us -> 32.6 us  [tree(): pl.pallas_call(tree_kernel, out_shape=(VMEM((HALF, RANK), BF16), VMEM((2,...]
where the time goes in v3:
time: 34.2 us; the launch traced here: 34 us
  Pallas kernels  34 us (99%)
    pallas_call x1, Pallas kernels, tree(): pl.pallas_call(tree_kernel, out_shape=(VMEM((HALF, RANK), BF16), VMEM((2,...  32.6 us
    pallas_call x1, Pallas kernels, far(): pl.pallas_call(far_kernel, out_shape=jax.ShapeDtypeStruct((ROWS, RHS), BF...  1.42 us

profile of v3, /device:TPU:1, one launch (start us, length us, event | category | flops | bytes accessed | tf_op | source)
XLA Modules:
  0.0 34.0 jit_solution(6066296501943770178)
XLA Ops:
  0.0 32.6 %tree.1 = (bf16[256,256]{1,0:T(8,128)(2,1)S(1)}, f32[2,2048,256]{2,1,0:T(8,128)S(1)}, bf16[2048,256]{1,0:T(8,128)(2,1)S(1)}, bf16[2048,256]{1,0:T(8,128)(2,1)S(1)}) custom-call(s32[16,128]{1,0:T(8,128)} %bitcast.4, s32[8,16]{1,0:T(8,128)} %bitcast.5, bf16[2048,512]{1,0:T(8,128)(2,1)} %sources_h.1, bf16[2048,256]{1,0:T(8,128)(2,1)} %basis_h.1, ...), custom_call_target="tpu_custom_call" | custom-call | tf_op jit(solution)/shard_map/tree/pallas_call | solution.py:382
  32.6 1.4 %far.1 = bf16[2048,512]{1,0:T(8,128)(2,1)} custom-call(bf16[2048,256]{1,0:T(8,128)(2,1)S(1)} %get-tuple-element.9.basis, bf16[256,256]{1,0:T(8,128)(2,1)S(1)} %get-tuple-element.10.other, f32[2,2048,256]{2,1,0:T(8,128)S(1)} %get-tuple-element.11.near, bf16[2048,256]{1,0:T(8,128)(2,1)S(1)} %get-tuple-element.12.own), custom_call_target="tpu_custom_call" | custom-call | tf_op jit(solution)/shard_map/far/pallas_call | solution.py:424

commit v4 on v3

--- a/solution.py
+++ b/solution.py
@@ -23,7 +23,6 @@
 HALF = RHS // 2
 PIECES = 4
 PIECE = QUARTER // PIECES
-GATHER_ROWS = 512
 OUT_ROWS = 512
 LAST_ROWS = 256
 SCATTER_ROWS = 1024
@@ -90,9 +89,9 @@
     for who in partners:
         pl.semaphore_signal(barrier, inc=1, device_id=who, device_id_type=MESH)
 
-    def remote(src, dst, i, p, who):
+    def remote(src, dst, i, j, who):
         return pltpu.make_async_remote_copy(
-            src_ref=src, dst_ref=dst, send_sem=send.at[i, p], recv_sem=recv.at[i, p],
+            src_ref=src, dst_ref=dst, send_sem=send.at[i], recv_sem=recv.at[j],
             device_id=who, device_id_type=MESH,
         )
 
@@ -137,7 +136,7 @@
     part_b[pl.ds(2 - 2 * half, 2)] = half_term(1 - half).astype(BF16).reshape(pair)
     send_c = [
         [
-            remote(part_b.at[k, piece(p)], part_in.at[i, piece(p)], 1 + i, p, who)
+            remote(part_b.at[k, piece(p)], part_in.at[i, piece(p)], 2, 4 + p, who)
             for i, (k, who) in enumerate(((q2, zside), (q3, cross), (q1, core)))
         ]
         for p in range(PIECES)
@@ -151,11 +150,11 @@
     for p in range(PIECES):
         send_c[p][2].start()
 
-    def gather(b, _):
+    def gather(k0, count):
         lanes = lax.broadcasted_iota(I32, (BLOCK, BLOCK), 1) + first_row
         rows = []
-        for k in range(GATHER_ROWS // BLOCK):
-            ids = order_col[b * (GATHER_ROWS // BLOCK) + k]
+        for k in range(count):
+            ids = order_col[k0 + k]
             rows.append(
                 jnp.concatenate(
                     [jnp.where(lanes + c * BLOCK == ids, 1.0, 0.0).astype(BF16) for c in range(BLOCKS_DEV)],
@@ -163,12 +162,11 @@
                 )
             )
         hot = jnp.concatenate(rows, axis=0)
-        at = pl.multiple_of(b * GATHER_ROWS + HALO, HALO)
-        permuted[pl.ds(at, GATHER_ROWS), :] = dot(hot, sources[...]).astype(BF16)
-        return 0
-
-    first = 3 - 3 * (n // 2)
-    gather(first, 0)
+        at = pl.multiple_of(k0 * BLOCK + HALO, BLOCK)
+        permuted[pl.ds(at, count * BLOCK), :] = dot(hot, sources[...]).astype(BF16)
+
+    first = (BLOCKS_DEV - REACH) * (1 - n // 2)
+    gather(first, REACH)
 
     def halo_copy(up):
         if up:
@@ -205,32 +203,33 @@
     table_copy = pltpu.make_async_copy(table_v, table_s, table_sem)
     table_copy.start()
 
+    gather(BLOCKS_DEV - REACH - first, REACH)
+
+    @pl.when(n == 2)
+    def _():
+        halo_copy(1).start()
+
+    @pl.when(n == 1)
+    def _():
+        halo_copy(0).start()
+
     send_x = []
     for p in range(PIECES):
-        for one in send_c[p]:
-            one.wait_recv()
+        remote(part_in.at[:, piece(p)], part_in.at[:, piece(p)], 2, 4 + p, core).wait_recv()
         own = part[quarter % 2, piece(p), :]
         for i in range(3):
             own = own + part_in[i, piece(p), :].astype(F32)
         c0[piece(p), :] = own.astype(BF16)
         send_x.append(
             [
-                remote(c0.at[piece(p)], x_in.at[i, piece(p)], 4 + i, p, who)
+                remote(c0.at[piece(p)], x_in.at[i, piece(p)], 3, 4 + PIECES + p, who)
                 for i, who in ((1, x2), (0, x1), (2, x3))
             ]
         )
         for one in send_x[p]:
             one.start()
-
-    gather(3 - first, 0)
-
-    @pl.when(n == 2)
-    def _():
-        halo_copy(1).start()
-
-    @pl.when(n == 1)
-    def _():
-        halo_copy(0).start()
+        if p < PIECES - 1:
+            gather(REACH + p, 1)
 
     @pl.when(n == 0)
     def _():
@@ -244,9 +243,10 @@
             permuted[at : at + BLOCK, :] = permuted[ROWS + HALO - BLOCK : ROWS + HALO, :]
 
     send_tx.wait_recv()
-    pass_tx = remote(transfer_x.at[side], transfer_x.at[side], 0, 1, core)
+    pass_tx = remote(transfer_x.at[side], transfer_x.at[side], 1, 1, core)
     pass_tx.start()
-    gather(1, 0)
+    gather(2 * REACH - 1, 1)
+    gather(2 * REACH, REACH)
     table_copy.wait()
     loads[5].wait()
 
@@ -271,25 +271,23 @@
         near_o[1, pl.ds(at, 2 * BLOCK), :] = found[:, HALF:]
         return 0
 
-    remote(transfer_x.at[1 - side], transfer_x.at[1 - side], 0, 1, core).wait_recv()
+    remote(transfer_x.at[1 - side], transfer_x.at[1 - side], 1, 1, core).wait_recv()
     send_h1 = []
     for p in range(PIECES):
-        for one in send_x[p]:
-            one.wait_recv()
+        remote(x_in.at[:, piece(p)], x_in.at[:, piece(p)], 3, 4 + PIECES + p, x1).wait_recv()
         c1 = level(c0[piece(p), :], x_in[0, piece(p), :], transfer[0])
         c1x = level(x_in[1, piece(p), :], x_in[2, piece(p), :], transfer_x[...])
         c2[piece(p), :] = level(c1, c1x, transfer[1])
-        send_h1.append(remote(c2.at[piece(p)], h1_in.at[piece(p)], 7, p, h1))
+        send_h1.append(remote(c2.at[piece(p)], h1_in.at[piece(p)], 4, 4 + 2 * PIECES + p, h1))
         send_h1[p].start()
 
-    gather(2, 0)
     lax.fori_loop(2, 5, near_pair, 0)
 
     send_h2 = []
     for p in range(PIECES):
         send_h1[p].wait_recv()
         c3[piece(p), :] = level(c2[piece(p), :], h1_in[piece(p), :], transfer[2])
-        send_h2.append(remote(c3.at[piece(p)], h2_in.at[piece(p)], 8, p, h2))
+        send_h2.append(remote(c3.at[piece(p)], h2_in.at[piece(p)], 5, 4 + 3 * PIECES + p, h2))
         send_h2[p].start()
 
     lax.fori_loop(5, 6, near_pair, 0)
@@ -307,7 +305,7 @@
     loads[6].wait()
 
     def share(i, k, p, who):
-        return remote(coarse.at[k, piece(p)], coarse.at[k, piece(p)], 9 + i, p, who)
+        return remote(coarse.at[k, piece(p)], coarse.at[k, piece(p)], 6, 2 + i // 2, who)
 
     send_q = []
     for p in range(PIECES):
@@ -316,8 +314,7 @@
         send_q += [share(i, quarter, p, who) for i, who in enumerate((zside, cross, core))]
         for one in send_q[-3:]:
             one.start()
-    for p in range(PIECES):
-        share(2, q1, p, core).wait_recv()
+    remote(coarse.at[q1], coarse.at[q1], 6, 3, core).wait_recv()
 
     held = coarse[pl.ds(2 * half, 2)].reshape(HALF, RANK)
 
@@ -330,8 +327,11 @@
 
     send_tx.wait_send()
     pass_tx.wait_send()
-    for one in (*sum(send_c, []), *sum(send_x, []), *send_h1, *send_h2, *send_q):
-        one.wait_send()
+    remote(part_in, part_in, 2, 4, core).wait_send()
+    remote(x_in, x_in, 3, 4, x1).wait_send()
+    remote(c2, h1_in, 4, 4, h1).wait_send()
+    remote(c3, h2_in, 5, 4, h2).wait_send()
+    remote(part_in, part_in, 6, 4, core).wait_send()
 
     @pl.when(n < 3)
     def _():
@@ -341,9 +341,8 @@
     def _():
         halo_copy(0).wait_send()
 
-    for p in range(PIECES):
-        share(0, q2, p, zside).wait_recv()
-        share(1, q3, p, cross).wait_recv()
+    far_half = coarse.at[pl.ds(2 - 2 * half, 2)]
+    remote(far_half, far_half, 6, 2, zside).wait_recv()
     other_o[...] = coarse[pl.ds(2 - 2 * half, 2)].reshape(HALF, RANK)
 
 
@@ -374,8 +373,8 @@
         VMEM((4, *quarter), BF16),
         DMA((7,)),
         DMA,
-        DMA((12, PIECES)),
-        DMA((12, PIECES)),
+        DMA((7,)),
+        DMA((4 + 4 * PIECES,)),
         DMA((2,)),
         DMA((2,)),
     ]

time: 34.2 us -> 33.3 us (0.974)
  Pallas kernels: 34 us -> 33.2 us
    pallas_call x1, Pallas kernels: 32.6 us -> 31.8 us  [tree(): pl.pallas_call(tree_kernel, out_shape=(VMEM((HALF, RANK), BF16), VMEM((2,...]
where the time goes in v4:
time: 33.3 us; the launch traced here: 33.2 us
  Pallas kernels  33.2 us (100%)
    pallas_call x1, Pallas kernels, tree(): pl.pallas_call(tree_kernel, out_shape=(VMEM((HALF, RANK), BF16), VMEM((2,...  31.8 us
    pallas_call x1, Pallas kernels, far(): pl.pallas_call(far_kernel, out_shape=jax.ShapeDtypeStruct((ROWS, RHS), BF...  1.42 us

profile of v4, /device:TPU:1, one launch (start us, length us, event | category | flops | bytes accessed | tf_op | source)
XLA Modules:
  0.0 33.2 jit_solution(10395589535172948361)
XLA Ops:
  0.0 31.8 %tree.1 = (bf16[256,256]{1,0:T(8,128)(2,1)S(1)}, f32[2,2048,256]{2,1,0:T(8,128)S(1)}, bf16[2048,256]{1,0:T(8,128)(2,1)S(1)}, bf16[2048,256]{1,0:T(8,128)(2,1)S(1)}) custom-call(s32[16,128]{1,0:T(8,128)} %bitcast.4, s32[8,16]{1,0:T(8,128)} %bitcast.5, bf16[2048,512]{1,0:T(8,128)(2,1)} %sources_h.1, bf16[2048,256]{1,0:T(8,128)(2,1)} %basis_h.1, ...), custom_call_target="tpu_custom_call" | custom-call | tf_op jit(solution)/shard_map/tree/pallas_call | solution.py:381
  31.8 1.4 %far.1 = bf16[2048,512]{1,0:T(8,128)(2,1)} custom-call(bf16[2048,256]{1,0:T(8,128)(2,1)S(1)} %get-tuple-element.9.basis, bf16[256,256]{1,0:T(8,128)(2,1)S(1)} %get-tuple-element.10.other, f32[2,2048,256]{2,1,0:T(8,128)S(1)} %get-tuple-element.11.near, bf16[2048,256]{1,0:T(8,128)(2,1)S(1)} %get-tuple-element.12.own), custom_call_target="tpu_custom_call" | custom-call | tf_op jit(solution)/shard_map/far/pallas_call | solution.py:423

commit v5 on v4

--- a/solution.py
+++ b/solution.py
@@ -281,7 +281,7 @@
         send_h1.append(remote(c2.at[piece(p)], h1_in.at[piece(p)], 4, 4 + 2 * PIECES + p, h1))
         send_h1[p].start()
 
-    lax.fori_loop(2, 5, near_pair, 0)
+    lax.fori_loop(2, 4, near_pair, 0)
 
     send_h2 = []
     for p in range(PIECES):
@@ -290,7 +290,7 @@
         send_h2.append(remote(c3.at[piece(p)], h2_in.at[piece(p)], 5, 4 + 3 * PIECES + p, h2))
         send_h2[p].start()
 
-    lax.fori_loop(5, 6, near_pair, 0)
+    lax.fori_loop(4, 6, near_pair, 0)
 
     @pl.when(n > 0)
     def _():

time: 33.3 us -> 34 us (1.021)
  Pallas kernels: 33.2 us -> 33.9 us
    pallas_call x1, Pallas kernels: 31.8 us -> 32.5 us  [tree(): pl.pallas_call(tree_kernel, out_shape=(VMEM((HALF, RANK), BF16), VMEM((2,...]
where the time goes in v5:
time: 34 us; the launch traced here: 33.9 us
  Pallas kernels  33.9 us (100%)
    pallas_call x1, Pallas kernels, tree(): pl.pallas_call(tree_kernel, out_shape=(VMEM((HALF, RANK), BF16), VMEM((2,...  32.5 us
    pallas_call x1, Pallas kernels, far(): pl.pallas_call(far_kernel, out_shape=jax.ShapeDtypeStruct((ROWS, RHS), BF...  1.42 us

profile of v5, /device:TPU:1, one launch (start us, length us, event | category | flops | bytes accessed | tf_op | source)
XLA Modules:
  0.0 33.9 jit_solution(2752796562867577778)
XLA Ops:
  0.0 32.5 %tree.1 = (bf16[256,256]{1,0:T(8,128)(2,1)S(1)}, f32[2,2048,256]{2,1,0:T(8,128)S(1)}, bf16[2048,256]{1,0:T(8,128)(2,1)S(1)}, bf16[2048,256]{1,0:T(8,128)(2,1)S(1)}) custom-call(s32[16,128]{1,0:T(8,128)} %bitcast.4, s32[8,16]{1,0:T(8,128)} %bitcast.5, bf16[2048,512]{1,0:T(8,128)(2,1)} %sources_h.1, bf16[2048,256]{1,0:T(8,128)(2,1)} %basis_h.1, ...), custom_call_target="tpu_custom_call" | custom-call | tf_op jit(solution)/shard_map/tree/pallas_call | solution.py:381
  32.5 1.4 %far.1 = bf16[2048,512]{1,0:T(8,128)(2,1)} custom-call(bf16[2048,256]{1,0:T(8,128)(2,1)S(1)} %get-tuple-element.9.basis, bf16[256,256]{1,0:T(8,128)(2,1)S(1)} %get-tuple-element.10.other, f32[2,2048,256]{2,1,0:T(8,128)S(1)} %get-tuple-element.11.near, bf16[2048,256]{1,0:T(8,128)(2,1)S(1)} %get-tuple-element.12.own), custom_call_target="tpu_custom_call" | custom-call | tf_op jit(solution)/shard_map/far/pallas_call | solution.py:423

commit v6 on v5

--- a/solution.py
+++ b/solution.py
@@ -281,7 +281,7 @@
         send_h1.append(remote(c2.at[piece(p)], h1_in.at[piece(p)], 4, 4 + 2 * PIECES + p, h1))
         send_h1[p].start()
 
-    lax.fori_loop(2, 4, near_pair, 0)
+    lax.fori_loop(2, 6, near_pair, 0)
 
     send_h2 = []
     for p in range(PIECES):
@@ -289,8 +289,6 @@
         c3[piece(p), :] = level(c2[piece(p), :], h1_in[piece(p), :], transfer[2])
         send_h2.append(remote(c3.at[piece(p)], h2_in.at[piece(p)], 5, 4 + 3 * PIECES + p, h2))
         send_h2[p].start()
-
-    lax.fori_loop(4, 6, near_pair, 0)
 
     @pl.when(n > 0)
     def _():

time: 34 us -> 33.5 us (0.985)
  Pallas kernels: 33.9 us -> 33.4 us
    pallas_call x1, Pallas kernels: 32.5 us -> 31.9 us  [tree(): pl.pallas_call(tree_kernel, out_shape=(VMEM((HALF, RANK), BF16), VMEM((2,...]
where the time goes in v6:
time: 33.5 us; the launch traced here: 33.4 us
  Pallas kernels  33.4 us (100%)
    pallas_call x1, Pallas kernels, tree(): pl.pallas_call(tree_kernel, out_shape=(VMEM((HALF, RANK), BF16), VMEM((2,...  31.9 us
    pallas_call x1, Pallas kernels, far(): pl.pallas_call(far_kernel, out_shape=jax.ShapeDtypeStruct((ROWS, RHS), BF...  1.42 us

profile of v6, /device:TPU:1, one launch (start us, length us, event | category | flops | bytes accessed | tf_op | source)
XLA Modules:
  0.0 33.4 jit_solution(18224997604588987362)
XLA Ops:
  0.0 31.9 %tree.1 = (bf16[256,256]{1,0:T(8,128)(2,1)S(1)}, f32[2,2048,256]{2,1,0:T(8,128)S(1)}, bf16[2048,256]{1,0:T(8,128)(2,1)S(1)}, bf16[2048,256]{1,0:T(8,128)(2,1)S(1)}) custom-call(s32[16,128]{1,0:T(8,128)} %bitcast.4, s32[8,16]{1,0:T(8,128)} %bitcast.5, bf16[2048,512]{1,0:T(8,128)(2,1)} %sources_h.1, bf16[2048,256]{1,0:T(8,128)(2,1)} %basis_h.1, ...), custom_call_target="tpu_custom_call" | custom-call | tf_op jit(solution)/shard_map/tree/pallas_call | solution.py:379
  32.0 1.4 %far.1 = bf16[2048,512]{1,0:T(8,128)(2,1)} custom-call(bf16[2048,256]{1,0:T(8,128)(2,1)S(1)} %get-tuple-element.9.basis, bf16[256,256]{1,0:T(8,128)(2,1)S(1)} %get-tuple-element.10.other, f32[2,2048,256]{2,1,0:T(8,128)S(1)} %get-tuple-element.11.near, bf16[2048,256]{1,0:T(8,128)(2,1)S(1)} %get-tuple-element.12.own), custom_call_target="tpu_custom_call" | custom-call | tf_op jit(solution)/shard_map/far/pallas_call | solution.py:421
